TPU v7x, 32 devices: a whole 2x2x4 slice. The times are simulated.
32 devices in a mesh: row: 8 (over z, x), col: 4 (over y, core).
Axes of the slice: x: 2, y: 2, z: 4, core: 2. Of those that a mesh axis runs over, the one named last changes fastest.
Arguments:
- records: bfloat16 [128, 8, 1500], P('row', 'col'), may hold values from -6 to 6
- channel_live: int32 [128], replicated, may hold values 0 or 1
- minute_valid: int32 [8], replicated, may hold values 0 or 1
Outputs:
- correlations: bfloat16 [128, 128, 801], P('row', 'col')
All inputs are finite; a program needn't handle non-finite values.
Results may differ from a plain program's by a relative error of at most 0.0075.
Values may be sent and summed in bfloat16 or wider, within the bound.
A program may use at most 64 MiB of HBM per device.

v0:
```python
import math
import jax
import jax.numpy as jnp
from jax import lax
from jax.sharding import PartitionSpec as P

F = 640
BAND = 32
MAXLAG = 400


def forward_table(length, nfreq):
    times = jnp.arange(length, dtype=jnp.int32)[:, None]
    freqs = jnp.arange(1, nfreq + 1, dtype=jnp.int32)[None, :]
    phase = (times * freqs % length).astype(jnp.float32) * jnp.float32(2.0 * math.pi / length)
    return jnp.concatenate([jnp.cos(phase), -jnp.sin(phase)], axis=1).astype(jnp.bfloat16)


def inverse_table(length, nfreq, maxlag):
    freqs = jnp.arange(1, nfreq + 1, dtype=jnp.int32)[:, None]
    shifts = jnp.arange(-maxlag, maxlag + 1, dtype=jnp.int32)[None, :]
    phase = jnp.mod(freqs * shifts, length).astype(jnp.float32) * jnp.float32(
        2.0 * math.pi / length
    )
    return jnp.concatenate([jnp.cos(phase), -jnp.sin(phase)], axis=0).astype(jnp.bfloat16)


def whiten(signal, live, valid, table, band):
    chans, mins, length = signal.shape
    nfreq = table.shape[1] // 2
    spectrum = jnp.dot(
        signal.reshape(chans * mins, length), table, preferred_element_type=jnp.float32
    )
    grouped = spectrum.reshape(chans, mins, 2, nfreq // band, band)
    power = jnp.mean(grouped * grouped, axis=(2, 4))
    weight = (
        lax.rsqrt(power + 1e-06)
        * live.astype(jnp.float32)[:, None, None]
        * valid.astype(jnp.float32)[None, :, None]
    )
    return (
        (grouped * weight[:, :, None, :, None]).reshape(chans, mins, 2 * nfreq).astype(jnp.bfloat16)
    )


def correlate(rows, cols, itab, count):
    nfreq = rows.shape[2] // 2
    row_real = rows[:, :, :nfreq]
    row_imag = rows[:, :, nfreq:]
    col_real = cols[:, :, :nfreq]
    col_imag = cols[:, :, nfreq:]
    real_sum = jnp.einsum(
        "imf,jmf->ijf", row_real, col_real, preferred_element_type=jnp.float32
    ) + jnp.einsum("imf,jmf->ijf", row_imag, col_imag, preferred_element_type=jnp.float32)
    imag_sum = jnp.einsum(
        "imf,jmf->ijf", row_imag, col_real, preferred_element_type=jnp.float32
    ) - jnp.einsum("imf,jmf->ijf", row_real, col_imag, preferred_element_type=jnp.float32)
    stacked = (jnp.concatenate([real_sum, imag_sum], axis=-1) / jnp.float32(count)).astype(
        jnp.bfloat16
    )
    lagged = jnp.dot(stacked.reshape(-1, 2 * nfreq), itab, preferred_element_type=jnp.float32)
    lagged = lagged * jnp.float32(1.0 / math.sqrt(nfreq))
    return lagged.astype(jnp.bfloat16).reshape(rows.shape[0], cols.shape[0], itab.shape[1])


def body(records, channel_live, minute_valid):
    row_total = lax.axis_size("row")
    col_total = lax.axis_size("col")
    row_count = records.shape[0]
    per_device = records.shape[1]
    length = records.shape[2]
    channels = row_count * row_total
    col_count = channels // col_total
    minutes = per_device * col_total
    col_index = lax.axis_index("col")
    row_start = lax.axis_index("row") * row_count
    row_live = lax.dynamic_slice_in_dim(channel_live, row_start, row_count)
    table = forward_table(length, F)
    own_valid = lax.dynamic_slice_in_dim(minute_valid, col_index * per_device, per_device)
    local = whiten(records, row_live, own_valid, table, BAND)
    row_spectra = lax.all_gather(local, "col", axis=1, tiled=True)
    every_channel = lax.all_gather(local, "row", axis=0, tiled=True)
    col_spectra = lax.all_to_all(every_channel, "col", split_axis=0, concat_axis=1, tiled=True)
    itab = inverse_table(length, F, MAXLAG)
    block = math.gcd(row_count, 8)
    grouped = row_spectra.reshape(row_count // block, block, minutes, 2 * F)

    def one_block(rows):
        return correlate(rows, col_spectra, itab, minutes)

    result = lax.map(one_block, grouped)
    return result.reshape(row_count, col_count, 2 * MAXLAG + 1)


def solution(mesh):
    in_specs = (P("row", "col", None), P(), P())
    out_specs = P("row", "col", None)
    return jax.shard_map(body, mesh=mesh, in_specs=in_specs, out_specs=out_specs, check_vma=False)
```

profile of v0, /device:TPU:0, one launch (start us, length us, event | category | flops | bytes accessed | tf_op | source)
XLA Modules:
  0.0 129.4 jit_solution(9751996412103795063)
XLA Ops:
  0.0 17.2 %cosine_convert_fusion = (bf16[1500,640]{1,0:T(8,128)(2,1)S(1)}, bf16[1500,640]{1,0:T(8,128)(2,1)}) fusion(s32[640]{0:T(1024)S(1)} %iota_add_fusion.1), kind=kLoop, calls=%fused_computation.31 | loop fusion | flops 11520000 | bytes 3842560 | tf_op jit(solution)/shard_map/convert.2
  17.2 0.0 copy-done.5
  17.2 0.1 reshape.42
  17.3 0.0 copy-start.8
  17.3 0.0 copy-start.9
  17.3 2.3 %fusion.45 = (f32[32,1280]{1,0:T(8,128)S(1)}, f32[32,1280]{1,0:T(8,128)S(1)}) fusion(bf16[32,1500]{1,0:T(8,128)(2,1)S(1)} %reshape.42, bf16[1500,640]{1,0:T(8,128)(2,1)} %get-tuple-element.61, bf16[1500,640]{1,0:T(8,128)(2,1)S(1)} %get-tuple-element.60), kind=kOutput, calls=%fused_computation.59 | convolution fusion | flops 130600960 | bytes 4263680 | tf_op jit(solution)/shard_map/dot_general | solution.py:31
  19.6 0.3 mul.110
  19.9 0.1 dynamic-slice_convert_fusion.1
  20.0 0.1 dynamic-slice_convert_fusion
  20.0 0.2 reduce_sum.9
  20.2 0.1 fusion.43
  20.3 0.2 mul.117
  20.5 0.3 mul.118
  20.8 0.1 reshape.43
  20.9 33.5 %all_gather.7 = bf16[128,2,1280]{2,0,1:T(8,128)(2,1)S(1)} all-gather(bf16[16,2,1280]{2,0,1:T(8,128)(2,1)S(1)} %fusion.39), channel_id=1, replica_groups=mesh['row'=8,'col'=4] {'row'}, dimensions={0}, use_global_device_ids=true | all-gather | bytes 737280 | tf_op jit(solution)/shard_map/all_gather | solution.py:82
  54.4 1.5 %copy.28 = bf16[128,2,1280]{2,1,0:T(2,128)(2,1)} copy(bf16[128,2,1280]{2,0,1:T(8,128)(2,1)S(1)} %all_gather.7) | data formatting | bytes 1310720 | tf_op jit(solution)/shard_map/all_gather | solution.py:82
  55.9 3.5 %all-to-all-start = ((bf16[128,2,1280]{2,1,0:T(2,128)(2,1)}), bf16[128,2,1280]{2,1,0:T(2,128)(2,1)S(1)}, u32[]{:S(2)}, u32[]{:S(2)}) async-start(bf16[128,2,1280]{2,1,0:T(2,128)(2,1)} %copy.28), calls=%async_computation | async-start | bytes 1310720 | tf_op jit(solution)/shard_map/all_to_all | solution.py:83
  59.4 10.2 %cosine_convert_fusion.1 = (bf16[640,801]{1,0:T(8,128)(2,1)S(1)}, bf16[640,801]{1,0:T(8,128)(2,1)S(1)}) fusion(s32[801]{0:T(1024)S(1)} %iota_add_fusion, s32[640]{0:T(1024)S(1)} %iota_add_fusion.1), kind=kLoop, calls=%fused_computation.41 | loop fusion | flops 6151680 | bytes 2056324 | tf_op jit(solution)/shard_map/convert
  69.6 6.8 %all_gather.6 = bf16[16,8,1280]{2,0,1:T(8,128)(2,1)S(1)} all-gather(bf16[16,2,1280]{2,0,1:T(8,128)(2,1)S(1)} %fusion.39), channel_id=1, replica_groups=mesh['row'=8,'col'=4] {'col'}, dimensions={1}, use_global_device_ids=true | all-gather | bytes 409600 | tf_op jit(solution)/shard_map/all_gather | solution.py:81
  76.4 1.6 %pad_maximum_fusion = bf16[1280,801]{1,0:T(8,128)(2,1)} fusion(bf16[640,801]{1,0:T(8,128)(2,1)S(1)} %get-tuple-element.59, bf16[640,801]{1,0:T(8,128)(2,1)S(1)} %get-tuple-element.58), kind=kLoop, calls=%fused_computation.39 | loop fusion | flops 4101120 | bytes 4101120 | tf_op jit(solution)/shard_map/concatenate | solution.py:25
  78.0 0.0 all-to-all-done
  78.0 4.9 %copy.29 = bf16[32,4,2,1280]{0,2,1,3:T(2,128)(2,1)} copy(bf16[32,4,2,1280]{3,2,0,1:T(2,128)(2,1)S(1)} %bitcast.75) | data formatting | bytes 1310720 | tf_op jit(solution)/shard_map/all_to_all | solution.py:83
  82.9 46.5 %while.10 = (s32[]{:T(128)}, bf16[2,8,32,801]{3,2,1,0:T(8,128)(2,1)}, bf16[2,8,8,1280]{3,1,0,2:T(8,128)(2,1)S(1)}, bf16[32,8,1280]{0,1,2:T(8,128)(2,1)}, bf16[1280,801]{1,0:T(8,128)(2,1)}, /*index=5*/s32[]{:T(128)}) while((s32[]{:T(128)}, bf16[2,8,32,801]{3,2,1,0:T(8,128)(2,1)}, bf16[2,8,8,1280]{3,1,0,2:T(8,128)(2,1)S(1)}, ...), condition=%wide.region_2.3_spmd, body=%wide.region_1.2_spmd.sunk | while | flops 537149952 | bytes 34353424 | solution.py:91
  82.9 0.8 copy-done.3
  83.7 1.8 %copy.50 = bf16[1,8,8,1280]{2,1,3,0:T(8,128)(2,1)S(1)} copy(bf16[1,8,8,1280]{3,1,0,2:T(8,128)(2,1)S(1)} %constant_dynamic-slice_fusion.2) | data formatting | bytes 327680 | tf_op jit(solution)/shard_map/while/body/jit(dynamic_index_in_dim)/dynamic_slice | solution.py:91
  85.4 1.4 %fusion.98 = bf16[32,8,640]{0,1,2:T(8,128)(2,1)S(1)} fusion(bf16[32,8,1280]{0,1,2:T(8,128)(2,1)} %get-tuple-element.110), kind=kLoop, calls=%fused_computation.15.clone.1.clone.1 | loop fusion | bytes 655360 | tf_op jit(solution)/shard_map/while/body/eval_jaxpr/imf,jmf->ijf/dot_general | solution.py:54
  86.8 0.0 copy-start
  86.8 0.8 fusion.99
  87.7 0.9 copy-done
  88.6 0.1 fusion.100
  88.7 2.4 %add_bitcast_fusion.2 = f32[8,32,640]{1,0,2:T(8,128)} fusion(f32[640,8,32]{2,1,0:T(8,128)S(1)} %fusion.99, bf16[1,8,8,1280]{2,1,3,0:T(8,128)(2,1)S(1)} %copy.50, bf16[32,8,640]{0,1,2:T(8,128)(2,1)S(1)} %fusion.100), kind=kOutput, calls=%fused_computation.9.clone.2 | convolution fusion | flops 2785280 | bytes 1802240 | tf_op jit(solution)/shard_map/while/body/eval_jaxpr/imf,jmf->ijf/dot_general | solution.py:52
  91.0 3.0 %copy.52 = f32[8,32,640]{2,1,0:T(8,128)} copy(f32[8,32,640]{1,0,2:T(8,128)} %add_bitcast_fusion.2) | data formatting | bytes 1310720 | tf_op jit(solution)/shard_map/while/body/eval_jaxpr/add | solution.py:52
  94.1 1.4 %fusion.95 = bf16[32,8,640]{0,1,2:T(8,128)(2,1)S(1)} fusion(bf16[32,8,1280]{0,1,2:T(8,128)(2,1)} %get-tuple-element.110), kind=kLoop, calls=%fused_computation.16.clone.1.clone.1 | loop fusion | bytes 655360 | tf_op jit(solution)/shard_map/while/body/eval_jaxpr/imf,jmf->ijf/dot_general | solution.py:55
  95.5 0.8 fusion.96
  96.3 0.9 copy-done.1
  97.2 0.1 fusion.97
  97.3 2.4 %subtract_bitcast_fusion.2 = f32[8,32,640]{1,0,2:T(8,128)} fusion(f32[640,8,32]{2,1,0:T(8,128)S(1)} %fusion.96, bf16[1,8,8,1280]{2,1,3,0:T(8,128)(2,1)S(1)} %copy.50, bf16[32,8,640]{0,1,2:T(8,128)(2,1)S(1)} %fusion.97), kind=kOutput, calls=%fused_computation.8.clone.2 | convolution fusion | flops 2785280 | bytes 1802240 | tf_op jit(solution)/shard_map/while/body/eval_jaxpr/imf,jmf->ijf/dot_general | solution.py:57
  99.7 2.5 %copy.51 = f32[8,32,640]{2,1,0:T(8,128)S(1)} copy(f32[8,32,640]{1,0,2:T(8,128)} %subtract_bitcast_fusion.2) | data formatting | bytes 1310720 | tf_op jit(solution)/shard_map/while/body/eval_jaxpr/sub | solution.py:55
  102.2 0.0 copy-start.6
  102.2 2.7 %fusion.101 = bf16[256,801]{0,1:T(8,128)(2,1)S(1)} fusion(bf16[1280,801]{1,0:T(8,128)(2,1)} %get-tuple-element.111, f32[256,640]{1,0:T(8,128)S(1)} %bitcast.73, f32[256,640]{1,0:T(8,128)S(1)} %bitcast.72), kind=kOutput, calls=%fused_computation.13.clone.1 | convolution fusion | flops 526336512 | bytes 3771392 | tf_op jit(solution)/shard_map/while/body/eval_jaxpr/dot_general | solution.py:61
  104.9 0.2 copy.53
  105.2 0.1 constant_dynamic-update-slice_fusion.2
  105.2 0.0 copy-start.7
  105.2 0.9 copy-done.7
  106.2 0.8 copy-done.3
  106.9 1.8 %copy.50 = bf16[1,8,8,1280]{2,1,3,0:T(8,128)(2,1)S(1)} copy(bf16[1,8,8,1280]{3,1,0,2:T(8,128)(2,1)S(1)} %constant_dynamic-slice_fusion.2) | data formatting | bytes 327680 | tf_op jit(solution)/shard_map/while/body/jit(dynamic_index_in_dim)/dynamic_slice | solution.py:91
  108.7 1.4 %fusion.98 = bf16[32,8,640]{0,1,2:T(8,128)(2,1)S(1)} fusion(bf16[32,8,1280]{0,1,2:T(8,128)(2,1)} %get-tuple-element.110), kind=kLoop, calls=%fused_computation.15.clone.1.clone.1 | loop fusion | bytes 655360 | tf_op jit(solution)/shard_map/while/body/eval_jaxpr/imf,jmf->ijf/dot_general | solution.py:54
  110.1 0.8 fusion.99
  110.9 0.9 copy-done
  111.8 0.1 fusion.100
  111.9 2.4 %add_bitcast_fusion.2 = f32[8,32,640]{1,0,2:T(8,128)} fusion(f32[640,8,32]{2,1,0:T(8,128)S(1)} %fusion.99, bf16[1,8,8,1280]{2,1,3,0:T(8,128)(2,1)S(1)} %copy.50, bf16[32,8,640]{0,1,2:T(8,128)(2,1)S(1)} %fusion.100), kind=kOutput, calls=%fused_computation.9.clone.2 | convolution fusion | flops 2785280 | bytes 1802240 | tf_op jit(solution)/shard_map/while/body/eval_jaxpr/imf,jmf->ijf/dot_general | solution.py:52
  114.3 3.0 %copy.52 = f32[8,32,640]{2,1,0:T(8,128)} copy(f32[8,32,640]{1,0,2:T(8,128)} %add_bitcast_fusion.2) | data formatting | bytes 1310720 | tf_op jit(solution)/shard_map/while/body/eval_jaxpr/add | solution.py:52
  117.3 1.4 %fusion.95 = bf16[32,8,640]{0,1,2:T(8,128)(2,1)S(1)} fusion(bf16[32,8,1280]{0,1,2:T(8,128)(2,1)} %get-tuple-element.110), kind=kLoop, calls=%fused_computation.16.clone.1.clone.1 | loop fusion | bytes 655360 | tf_op jit(solution)/shard_map/while/body/eval_jaxpr/imf,jmf->ijf/dot_general | solution.py:55
  118.7 0.8 fusion.96
  119.6 0.9 copy-done.1
  120.5 0.1 fusion.97
  120.6 2.4 %subtract_bitcast_fusion.2 = f32[8,32,640]{1,0,2:T(8,128)} fusion(f32[640,8,32]{2,1,0:T(8,128)S(1)} %fusion.96, bf16[1,8,8,1280]{2,1,3,0:T(8,128)(2,1)S(1)} %copy.50, bf16[32,8,640]{0,1,2:T(8,128)(2,1)S(1)} %fusion.97), kind=kOutput, calls=%fused_computation.8.clone.2 | convolution fusion | flops 2785280 | bytes 1802240 | tf_op jit(solution)/shard_map/while/body/eval_jaxpr/imf,jmf->ijf/dot_general | solution.py:57
  122.9 2.5 %copy.51 = f32[8,32,640]{2,1,0:T(8,128)S(1)} copy(f32[8,32,640]{1,0,2:T(8,128)} %subtract_bitcast_fusion.2) | data formatting | bytes 1310720 | tf_op jit(solution)/shard_map/while/body/eval_jaxpr/sub | solution.py:55
  125.4 0.0 copy-start.6
  125.5 2.7 %fusion.101 = bf16[256,801]{0,1:T(8,128)(2,1)S(1)} fusion(bf16[1280,801]{1,0:T(8,128)(2,1)} %get-tuple-element.111, f32[256,640]{1,0:T(8,128)S(1)} %bitcast.73, f32[256,640]{1,0:T(8,128)S(1)} %bitcast.72), kind=kOutput, calls=%fused_computation.13.clone.1 | convolution fusion | flops 526336512 | bytes 3771392 | tf_op jit(solution)/shard_map/while/body/eval_jaxpr/dot_general | solution.py:61
  128.2 0.2 copy.53
  128.4 0.1 constant_dynamic-update-slice_fusion.2
  128.5 0.0 copy-start.7
  128.5 0.9 copy-done.7
  (24 shorter events, 0.1 us)
Async XLA Ops:
  0.0 17.2 %copy-start.5 = (bf16[16,2,1500]{2,1,0:T(2,128)(2,1)S(1)}, bf16[16,2,1500]{2,1,0:T(2,128)(2,1)}, u32[]{:S(2)}) copy-start(bf16[16,2,1500]{2,1,0:T(2,128)(2,1)} %param.5) | copy-start | bytes 288004
  17.3 2.6 %copy-start.8 = (s32[128]{0:T(128)S(1)}, s32[128]{0:T(128)}, u32[]{:S(2)}) copy-start(s32[128]{0:T(128)} %param.6) | copy-start | bytes 1540
  17.3 2.7 %copy-start.9 = (s32[8]{0:T(128)S(1)}, s32[8]{0:T(128)}, u32[]{:S(2)}) copy-start(s32[8]{0:T(128)} %param.7) | copy-start | bytes 100
  55.9 22.1 %all-to-all-start = ((bf16[128,2,1280]{2,1,0:T(2,128)(2,1)}), bf16[128,2,1280]{2,1,0:T(2,128)(2,1)S(1)}, u32[]{:S(2)}, u32[]{:S(2)}) async-start(bf16[128,2,1280]{2,1,0:T(2,128)(2,1)} %copy.28), calls=%async_computation | async-start | bytes 1310720 | tf_op jit(solution)/shard_map/all_to_all | solution.py:83
  82.9 0.8 copy-start.3
  86.8 1.7 %copy-start = (bf16[32,8,1280]{0,1,2:T(8,128)(2,1)S(1)}, bf16[32,8,1280]{0,1,2:T(8,128)(2,1)}, u32[]{:S(2)}) copy-start(bf16[32,8,1280]{0,1,2:T(8,128)(2,1)} %get-tuple-element.110) | copy-start | bytes 1966084 | tf_op jit(solution)/shard_map/while
  95.5 1.7 %copy-start.1 = (bf16[32,8,1280]{0,1,2:T(8,128)(2,1)S(1)}, bf16[32,8,1280]{0,1,2:T(8,128)(2,1)}, u32[]{:S(2)}) copy-start(bf16[32,8,1280]{0,1,2:T(8,128)(2,1)} %get-tuple-element.110) | copy-start | bytes 1966084 | tf_op jit(solution)/shard_map/while
  99.7 2.5 %copy-start.2 = (f32[8,32,640]{2,1,0:T(8,128)S(1)}, f32[8,32,640]{2,1,0:T(8,128)}, u32[]{:S(2)}) copy-start(f32[8,32,640]{2,1,0:T(8,128)} %copy.52) | copy-start | bytes 1966084 | tf_op jit(solution)/shard_map/while
  102.2 3.0 %copy-start.6 = (bf16[2,8,32,801]{3,2,1,0:T(8,128)(2,1)S(1)}, bf16[2,8,32,801]{3,2,1,0:T(8,128)(2,1)}, u32[]{:S(2)}) copy-start(bf16[2,8,32,801]{3,2,1,0:T(8,128)(2,1)} %get-tuple-element.102) | copy-start | bytes 2460676 | tf_op jit(solution)/shard_map/while
  102.2 4.0 %copy-start.4 = (bf16[2,8,8,1280]{3,1,0,2:T(8,128)(2,1)S(1)}, bf16[2,8,8,1280]{3,1,0,2:T(8,128)(2,1)}, u32[]{:S(2)}) copy-start(bf16[2,8,8,1280]{3,1,0,2:T(8,128)(2,1)} %copy-done.3) | copy-start | bytes 983044 | tf_op jit(solution)/shard_map/while
  105.2 0.9 copy-start.7
  106.2 0.8 copy-start.3
  110.1 1.7 %copy-start = (bf16[32,8,1280]{0,1,2:T(8,128)(2,1)S(1)}, bf16[32,8,1280]{0,1,2:T(8,128)(2,1)}, u32[]{:S(2)}) copy-start(bf16[32,8,1280]{0,1,2:T(8,128)(2,1)} %get-tuple-element.110) | copy-start | bytes 1966084 | tf_op jit(solution)/shard_map/while
  118.7 1.7 %copy-start.1 = (bf16[32,8,1280]{0,1,2:T(8,128)(2,1)S(1)}, bf16[32,8,1280]{0,1,2:T(8,128)(2,1)}, u32[]{:S(2)}) copy-start(bf16[32,8,1280]{0,1,2:T(8,128)(2,1)} %get-tuple-element.110) | copy-start | bytes 1966084 | tf_op jit(solution)/shard_map/while
  122.9 2.5 %copy-start.2 = (f32[8,32,640]{2,1,0:T(8,128)S(1)}, f32[8,32,640]{2,1,0:T(8,128)}, u32[]{:S(2)}) copy-start(f32[8,32,640]{2,1,0:T(8,128)} %copy.52) | copy-start | bytes 1966084 | tf_op jit(solution)/shard_map/while
  125.4 3.0 %copy-start.6 = (bf16[2,8,32,801]{3,2,1,0:T(8,128)(2,1)S(1)}, bf16[2,8,32,801]{3,2,1,0:T(8,128)(2,1)}, u32[]{:S(2)}) copy-start(bf16[2,8,32,801]{3,2,1,0:T(8,128)(2,1)} %get-tuple-element.102) | copy-start | bytes 2460676 | tf_op jit(solution)/shard_map/while
  125.4 4.0 %copy-start.4 = (bf16[2,8,8,1280]{3,1,0,2:T(8,128)(2,1)S(1)}, bf16[2,8,8,1280]{3,1,0,2:T(8,128)(2,1)}, u32[]{:S(2)}) copy-start(bf16[2,8,8,1280]{3,1,0,2:T(8,128)(2,1)} %copy-done.3) | copy-start | bytes 983044 | tf_op jit(solution)/shard_map/while
  128.5 0.9 copy-start.7
where the time goes:
time: 130 us; the launch traced here: 129 us
  blocking collectives  40.2 us (31%)
  local copies, waits for them, and re-layouts  35.4 us (27%)
  other arithmetic  29.5 us (23%)
  matrix products  20.4 us (16%)
  starting transfers between devices  3.48 us (3%)
    all_gather x1, blocking collectives, body(): every_channel = lax.all_gather(local, 'row', axis=0, tiled=True)  33.5 us
    another operation x2, other arithmetic  27.4 us
    while x28, local copies, waits for them, and re-layouts  7.03 us
    all_gather x1, blocking collectives, body(): row_spectra = lax.all_gather(local, 'col', axis=1, tiled=True)  6.76 us
    add x2, local copies, waits for them, and re-layouts, correlate(): jnp.einsum('imf,jmf->ijf', row_real, col_real, preferred_element_type=jnp...  6.06 us
    dot_general x2, matrix products, correlate(): jnp.dot(stacked.reshape(-1, 2 * nfreq), itab, preferred_element_type=jnp....  5.41 us
    sub x2, local copies, waits for them, and re-layouts, correlate(): jnp.einsum('imf,jmf->ijf', row_imag, col_real, preferred_element_type=jnp...  4.94 us
    all_to_all x1, local copies, waits for them, and re-layouts, body(): lax.all_to_all(every_channel, 'col', split_axis=0, concat_axis=1, tiled=T...  4.91 us
  transfers between devices with their start and end apart: 1, of which 0 were waited for; matrix products, arithmetic and copies ran while one was open for 9% of the time, Pallas kernels for 0%

commit v1 on v0

--- a/solution.py
+++ b/solution.py
@@ -7,6 +7,26 @@
 F = 640
 BAND = 32
 MAXLAG = 400
+
+
+def process_blocks(slab_in):
+    local_next, current_arr = (jax.lax.axis_size("col"), jax.lax.axis_index("col"))
+    m_next = list(slab_in.shape)
+    big = slab_in.shape[0] // local_next
+    m_next[0] = big
+    arr_out = m_next[1]
+    m_next[1] = arr_out * local_next
+    carry = jnp.zeros(m_next, slab_in.dtype)
+    for dev_j in range(local_next):
+        prior = lax.dynamic_slice_in_dim(slab_in, (current_arr ^ dev_j) * big, big, axis=0)
+        if dev_j:
+            prior = jax.lax.ppermute(
+                prior, "col", tuple(((dd, dd ^ dev_j) for dd in range(local_next)))
+            )
+        carry = lax.dynamic_update_slice_in_dim(
+            carry, prior, (current_arr ^ dev_j) * arr_out, axis=1
+        )
+    return carry
 
 
 def forward_table(length, nfreq):
@@ -80,7 +100,7 @@
     local = whiten(records, row_live, own_valid, table, BAND)
     row_spectra = lax.all_gather(local, "col", axis=1, tiled=True)
     every_channel = lax.all_gather(local, "row", axis=0, tiled=True)
-    col_spectra = lax.all_to_all(every_channel, "col", split_axis=0, concat_axis=1, tiled=True)
+    col_spectra = process_blocks(every_channel)
     itab = inverse_table(length, F, MAXLAG)
     block = math.gcd(row_count, 8)
     grouped = row_spectra.reshape(row_count // block, block, minutes, 2 * F)

time: 130 us -> 142 us (1.092)
  local copies, waits for them, and re-layouts: 35.4 us -> 46.4 us
  matrix products: 20.4 us -> 22.4 us
  starting transfers between devices: 3.48 us -> 1.86 us
    all_to_all x1 -> x0, local copies, waits for them, and re-layouts: 4.91 us -> none  [body(): lax.all_to_all(every_channel, 'col', split_axis=0, concat_axis=1, tiled=T...]
    ppermute x0 -> x3, local copies, waits for them, and re-layouts: none -> 4.03 us  [process_blocks(): jax.lax.ppermute(prior, 'col', tuple(((dd, dd ^ dev_j) for dd in range(lo...]
    while x28 -> x12, local copies, waits for them, and re-layouts: 7.03 us -> 3.04 us
    dynamic_update_slice x0 -> x4, local copies, waits for them, and re-layouts: none -> 3.84 us  [process_blocks(): lax.dynamic_update_slice_in_dim(carry, prior, (current_arr ^ dev_j) * arr...]
    all_to_all x1 -> x0, starting transfers between devices: 3.48 us -> none  [body(): lax.all_to_all(every_channel, 'col', split_axis=0, concat_axis=1, tiled=T...]
    dot_general x2, local copies, waits for them, and re-layouts: 0.17 us -> 2.81 us  [correlate(): jnp.einsum('imf,jmf->ijf', row_real, col_imag, preferred_element_type=jnp...]
    dot_general x2, local copies, waits for them, and re-layouts: 0.17 us -> 2.8 us  [correlate(): jnp.einsum('imf,jmf->ijf', row_real, col_real, preferred_element_type=jnp...]
    convert_element_type x2, local copies, waits for them, and re-layouts: 0.49 us -> 2.5 us  [correlate(): lagged.astype(jnp.bfloat16)]
  transfers between devices with their start and end apart: 1 -> 3, of which waited for: 0 -> 0; matrix products, arithmetic and copies ran while one was open for 9% -> 13% of each run, Pallas kernels for 0% -> 0%
where the time goes in v1:
time: 142 us; the launch traced here: 141 us
  local copies, waits for them, and re-layouts  46.4 us (33%)
  blocking collectives  40.4 us (28%)
  other arithmetic  29.5 us (21%)
  matrix products  22.4 us (16%)
  starting transfers between devices  1.86 us (1%)
    all_gather x1, blocking collectives, body(): every_channel = lax.all_gather(local, 'row', axis=0, tiled=True)  33.6 us
    another operation x2, other arithmetic  27.4 us
    dot_general x2, matrix products, correlate(): jnp.dot(stacked.reshape(-1, 2 * nfreq), itab, preferred_element_type=jnp....  7.41 us
    all_gather x1, blocking collectives, body(): row_spectra = lax.all_gather(local, 'col', axis=1, tiled=True)  6.79 us
    sub x2, local copies, waits for them, and re-layouts, correlate(): jnp.einsum('imf,jmf->ijf', row_imag, col_real, preferred_element_type=jnp...  6.25 us
    add x2, local copies, waits for them, and re-layouts, correlate(): jnp.einsum('imf,jmf->ijf', row_real, col_real, preferred_element_type=jnp...  6.08 us
    dynamic_slice x4, local copies, waits for them, and re-layouts, body(): result = lax.map(one_block, grouped)  5.37 us
    dot_general x2, matrix products, correlate(): jnp.einsum('imf,jmf->ijf', row_real, col_imag, preferred_element_type=jnp...  4.73 us
  transfers between devices with their start and end apart: 3, of which 0 were waited for; matrix products, arithmetic and copies ran while one was open for 13% of the time, Pallas kernels for 0%

profile of v1, /device:TPU:0, one launch (start us, length us, event | category | flops | bytes accessed | tf_op | source)
XLA Modules:
  0.0 140.8 jit_solution(2500571104201167020)
XLA Ops:
  0.0 17.2 %cosine_convert_fusion = (bf16[1500,640]{1,0:T(8,128)(2,1)S(1)}, bf16[1500,640]{1,0:T(8,128)(2,1)}) fusion(s32[640]{0:T(1024)S(1)} %iota_add_fusion.1), kind=kLoop, calls=%fused_computation.31 | loop fusion | flops 11520000 | bytes 3842560 | tf_op jit(solution)/shard_map/convert.2
  17.2 0.1 reshape.42
  17.3 0.0 copy-start.4
  17.3 0.0 copy-start.5
  17.3 2.3 %fusion.45 = (f32[32,1280]{1,0:T(8,128)S(1)}, f32[32,1280]{1,0:T(8,128)S(1)}) fusion(bf16[32,1500]{1,0:T(8,128)(2,1)S(1)} %reshape.42, bf16[1500,640]{1,0:T(8,128)(2,1)} %get-tuple-element.70, bf16[1500,640]{1,0:T(8,128)(2,1)S(1)} %get-tuple-element.69), kind=kOutput, calls=%fused_computation.67 | convolution fusion | flops 130600960 | bytes 4263680 | tf_op jit(solution)/shard_map/dot_general | solution.py:51
  19.6 0.3 mul.132
  19.9 0.1 dynamic-slice_convert_fusion
  20.0 0.1 dynamic-slice_convert_fusion.1
  20.0 0.2 reduce_sum.9
  20.2 0.1 fusion.43
  20.3 0.2 mul.139
  20.5 0.3 mul.140
  20.8 0.1 reshape.43
  20.9 33.6 %all_gather.7 = bf16[128,2,1280]{2,0,1:T(8,128)(2,1)S(1)} all-gather(bf16[16,2,1280]{2,0,1:T(8,128)(2,1)S(1)} %fusion.39), channel_id=1, replica_groups=mesh['row'=8,'col'=4] {'row'}, dimensions={0}, use_global_device_ids=true | all-gather | bytes 737280 | tf_op jit(solution)/shard_map/all_gather | solution.py:102
  54.5 0.8 constant_dynamic-slice_fusion.1
  55.2 1.5 %collective-permute-start.1 = (bf16[32,2,1280]{2,0,1:T(8,128)(2,1)}, bf16[32,2,1280]{2,0,1:T(8,128)(2,1)}, u32[]{:S(2)}, u32[]{:S(2)}) collective-permute-start(bf16[32,2,1280]{2,0,1:T(8,128)(2,1)} %get-tuple-element.64), channel_id=1, source_target_pairs={{0,2},{1,3},{2,0},{3,1},{4,6},{5,7},{6,4},{7,5},{8,10},{9,11},{10,... | collective-permute-start | bytes 491528 | tf_op jit(solution)/shard_map/ppermute | solution.py:23
  56.7 0.3 collective-permute-start.2
  57.1 0.5 copy.41
  57.6 10.2 %cosine_convert_fusion.1 = (bf16[640,801]{1,0:T(8,128)(2,1)S(1)}, bf16[640,801]{1,0:T(8,128)(2,1)S(1)}) fusion(s32[801]{0:T(1024)S(1)} %iota_add_fusion, s32[640]{0:T(1024)S(1)} %iota_add_fusion.1), kind=kLoop, calls=%fused_computation.41 | loop fusion | flops 6151680 | bytes 2056324 | tf_op jit(solution)/shard_map/convert
  67.8 1.6 %pad_maximum_fusion = bf16[1280,801]{1,0:T(8,128)(2,1)} fusion(bf16[640,801]{1,0:T(8,128)(2,1)S(1)} %get-tuple-element.68, bf16[640,801]{1,0:T(8,128)(2,1)S(1)} %get-tuple-element.67), kind=kLoop, calls=%fused_computation.39 | loop fusion | flops 4101120 | bytes 4101120 | tf_op jit(solution)/shard_map/concatenate | solution.py:45
  69.4 0.4 broadcast_in_dim.8
  69.8 1.0 constant_dynamic-update-slice_fusion.4
  70.7 6.8 %all_gather.6 = bf16[16,8,1280]{2,0,1:T(8,128)(2,1)} all-gather(bf16[16,2,1280]{2,0,1:T(8,128)(2,1)S(1)} %fusion.39), channel_id=1, replica_groups=mesh['row'=8,'col'=4] {'col'}, dimensions={1}, use_global_device_ids=true | all-gather | bytes 409600 | tf_op jit(solution)/shard_map/all_gather | solution.py:101
  77.5 1.3 copy.42
  78.9 1.0 constant_dynamic-update-slice_fusion.3
  79.8 0.0 collective-permute-done.1
  79.9 1.3 copy.43
  81.2 1.0 constant_dynamic-update-slice_fusion.2
  82.2 0.0 collective-permute-done.2
  82.2 1.3 copy.44
  83.5 1.0 constant_dynamic-update-slice_fusion.1
  84.5 56.3 %while.10 = (s32[]{:T(128)}, bf16[2,8,32,801]{3,2,1,0:T(8,128)(2,1)}, bf16[2,8,8,1280]{3,1,0,2:T(8,128)(2,1)}, bf16[32,8,1280]{0,1,2:T(8,128)(2,1)S(1)}, bf16[1280,801]{1,0:T(8,128)(2,1)}, /*index=5*/s32[]{:T(128)}) while((s32[]{:T(128)}, bf16[2,8,32,801]{3,2,1,0:T(8,128)(2,1)}, bf16[2,8,8,1280]{3,1,0,2:T(8,128)(2,1)}, ...), condition=%wide.region_2.3_spmd, body=%wide.region_1.2_spmd.sunk | while | flops 537149952 | bytes 25121948 | solution.py:111
  84.5 1.5 %copy-done = bf16[32,8,1280]{0,1,2:T(8,128)(2,1)} copy-done((bf16[32,8,1280]{0,1,2:T(8,128)(2,1)}, bf16[32,8,1280]{0,1,2:T(8,128)(2,1)S(1)}, u32[]{:S(2)}) %copy-start) | copy-done | bytes 655384 | tf_op jit(solution)/shard_map/while
  86.0 0.9 constant_dynamic-slice_fusion.6
  87.0 1.8 %copy.65 = bf16[1,8,8,1280]{2,1,3,0:T(8,128)(2,1)S(1)} copy(bf16[1,8,8,1280]{3,1,0,2:T(8,128)(2,1)S(1)} %constant_dynamic-slice_fusion.6) | data formatting | bytes 327680 | tf_op jit(solution)/shard_map/while/body/jit(dynamic_index_in_dim)/dynamic_slice | solution.py:111
  88.7 1.4 fusion.98
  90.1 0.8 fusion.99
  91.0 1.4 fusion.100
  92.4 2.4 %add_bitcast_fusion.2 = f32[8,32,640]{1,0,2:T(8,128)} fusion(f32[640,8,32]{2,1,0:T(8,128)S(1)} %fusion.99, bf16[1,8,8,1280]{2,1,3,0:T(8,128)(2,1)S(1)} %copy.65, bf16[32,8,640]{0,1,2:T(8,128)(2,1)S(1)} %fusion.100), kind=kOutput, calls=%fused_computation.9.clone.2 | convolution fusion | flops 2785280 | bytes 1802240 | tf_op jit(solution)/shard_map/while/body/eval_jaxpr/imf,jmf->ijf/dot_general | solution.py:72
  94.7 3.0 %copy.67 = f32[8,32,640]{2,1,0:T(8,128)} copy(f32[8,32,640]{1,0,2:T(8,128)} %add_bitcast_fusion.2) | data formatting | bytes 1310720 | tf_op jit(solution)/shard_map/while/body/eval_jaxpr/add | solution.py:72
  97.8 1.4 fusion.95
  99.2 0.8 fusion.96
  100.0 1.4 fusion.97
  101.4 2.4 %subtract_bitcast_fusion.2 = f32[8,32,640]{1,0,2:T(8,128)} fusion(f32[640,8,32]{2,1,0:T(8,128)S(1)} %fusion.96, bf16[1,8,8,1280]{2,1,3,0:T(8,128)(2,1)S(1)} %copy.65, bf16[32,8,640]{0,1,2:T(8,128)(2,1)S(1)} %fusion.97), kind=kOutput, calls=%fused_computation.8.clone.2 | convolution fusion | flops 2785280 | bytes 1802240 | tf_op jit(solution)/shard_map/while/body/eval_jaxpr/imf,jmf->ijf/dot_general | solution.py:77
  103.8 3.1 %copy.66 = f32[8,32,640]{2,1,0:T(8,128)} copy(f32[8,32,640]{1,0,2:T(8,128)} %subtract_bitcast_fusion.2) | data formatting | bytes 1310720 | tf_op jit(solution)/shard_map/while/body/eval_jaxpr/sub | solution.py:75
  106.9 3.7 %fusion.101 = bf16[256,801]{0,1:T(8,128)(2,1)} fusion(bf16[1280,801]{1,0:T(8,128)(2,1)} %get-tuple-element.120, f32[256,640]{1,0:T(8,128)} %bitcast.68, f32[256,640]{1,0:T(8,128)S(1)} %bitcast.67), kind=kOutput, calls=%fused_computation.13.clone.1 | convolution fusion | flops 526336512 | bytes 3771392 | tf_op jit(solution)/shard_map/while/body/eval_jaxpr/dot_general | solution.py:81
  110.6 1.2 copy.68
  111.9 0.8 constant_dynamic-update-slice_fusion.6
  112.7 1.5 %copy-done = bf16[32,8,1280]{0,1,2:T(8,128)(2,1)} copy-done((bf16[32,8,1280]{0,1,2:T(8,128)(2,1)}, bf16[32,8,1280]{0,1,2:T(8,128)(2,1)S(1)}, u32[]{:S(2)}) %copy-start) | copy-done | bytes 655384 | tf_op jit(solution)/shard_map/while
  114.2 0.9 constant_dynamic-slice_fusion.6
  115.1 1.8 %copy.65 = bf16[1,8,8,1280]{2,1,3,0:T(8,128)(2,1)S(1)} copy(bf16[1,8,8,1280]{3,1,0,2:T(8,128)(2,1)S(1)} %constant_dynamic-slice_fusion.6) | data formatting | bytes 327680 | tf_op jit(solution)/shard_map/while/body/jit(dynamic_index_in_dim)/dynamic_slice | solution.py:111
  116.9 1.4 fusion.98
  118.3 0.8 fusion.99
  119.1 1.4 fusion.100
  120.5 2.4 %add_bitcast_fusion.2 = f32[8,32,640]{1,0,2:T(8,128)} fusion(f32[640,8,32]{2,1,0:T(8,128)S(1)} %fusion.99, bf16[1,8,8,1280]{2,1,3,0:T(8,128)(2,1)S(1)} %copy.65, bf16[32,8,640]{0,1,2:T(8,128)(2,1)S(1)} %fusion.100), kind=kOutput, calls=%fused_computation.9.clone.2 | convolution fusion | flops 2785280 | bytes 1802240 | tf_op jit(solution)/shard_map/while/body/eval_jaxpr/imf,jmf->ijf/dot_general | solution.py:72
  122.9 3.0 %copy.67 = f32[8,32,640]{2,1,0:T(8,128)} copy(f32[8,32,640]{1,0,2:T(8,128)} %add_bitcast_fusion.2) | data formatting | bytes 1310720 | tf_op jit(solution)/shard_map/while/body/eval_jaxpr/add | solution.py:72
  125.9 1.4 fusion.95
  127.3 0.8 fusion.96
  128.2 1.4 fusion.97
  129.6 2.4 %subtract_bitcast_fusion.2 = f32[8,32,640]{1,0,2:T(8,128)} fusion(f32[640,8,32]{2,1,0:T(8,128)S(1)} %fusion.96, bf16[1,8,8,1280]{2,1,3,0:T(8,128)(2,1)S(1)} %copy.65, bf16[32,8,640]{0,1,2:T(8,128)(2,1)S(1)} %fusion.97), kind=kOutput, calls=%fused_computation.8.clone.2 | convolution fusion | flops 2785280 | bytes 1802240 | tf_op jit(solution)/shard_map/while/body/eval_jaxpr/imf,jmf->ijf/dot_general | solution.py:77
  131.9 3.1 %copy.66 = f32[8,32,640]{2,1,0:T(8,128)} copy(f32[8,32,640]{1,0,2:T(8,128)} %subtract_bitcast_fusion.2) | data formatting | bytes 1310720 | tf_op jit(solution)/shard_map/while/body/eval_jaxpr/sub | solution.py:75
  135.1 3.7 %fusion.101 = bf16[256,801]{0,1:T(8,128)(2,1)} fusion(bf16[1280,801]{1,0:T(8,128)(2,1)} %get-tuple-element.120, f32[256,640]{1,0:T(8,128)} %bitcast.68, f32[256,640]{1,0:T(8,128)S(1)} %bitcast.67), kind=kOutput, calls=%fused_computation.13.clone.1 | convolution fusion | flops 526336512 | bytes 3771392 | tf_op jit(solution)/shard_map/while/body/eval_jaxpr/dot_general | solution.py:81
  138.8 1.2 copy.68
  140.0 0.8 constant_dynamic-update-slice_fusion.6
  (20 shorter events, 0.1 us)
Async XLA Ops:
  0.0 17.2 %copy-start.3 = (bf16[16,2,1500]{2,1,0:T(2,128)(2,1)S(1)}, bf16[16,2,1500]{2,1,0:T(2,128)(2,1)}, u32[]{:S(2)}) copy-start(bf16[16,2,1500]{2,1,0:T(2,128)(2,1)} %param.5) | copy-start | bytes 288004
  17.3 2.6 %copy-start.4 = (s32[8]{0:T(128)S(1)}, s32[8]{0:T(128)}, u32[]{:S(2)}) copy-start(s32[8]{0:T(128)} %param.7) | copy-start | bytes 100
  17.3 2.7 %copy-start.5 = (s32[128]{0:T(128)S(1)}, s32[128]{0:T(128)}, u32[]{:S(2)}) copy-start(s32[128]{0:T(128)} %param.6) | copy-start | bytes 1540
  55.2 22.3 %collective-permute-start = (bf16[32,2,1280]{2,0,1:T(8,128)(2,1)}, bf16[32,2,1280]{2,0,1:T(8,128)(2,1)}, u32[]{:S(2)}, u32[]{:S(2)}) collective-permute-start(bf16[32,2,1280]{2,0,1:T(8,128)(2,1)} %get-tuple-element.65), channel_id=1, source_target_pairs={{0,1},{1,0},{2,3},{3,2},{4,5},{5,4},{6,7},{7,6},{8,9},{9,8},{10,11... | collective-permute-start | bytes 491528 | tf_op jit(solution)/shard_map/ppermute | solution.py:23
  55.2 24.6 %collective-permute-start.1 = (bf16[32,2,1280]{2,0,1:T(8,128)(2,1)}, bf16[32,2,1280]{2,0,1:T(8,128)(2,1)}, u32[]{:S(2)}, u32[]{:S(2)}) collective-permute-start(bf16[32,2,1280]{2,0,1:T(8,128)(2,1)} %get-tuple-element.64), channel_id=1, source_target_pairs={{0,2},{1,3},{2,0},{3,1},{4,6},{5,7},{6,4},{7,5},{8,10},{9,11},{10,... | collective-permute-start | bytes 491528 | tf_op jit(solution)/shard_map/ppermute | solution.py:23
  56.7 25.4 %collective-permute-start.2 = (bf16[32,2,1280]{2,0,1:T(8,128)(2,1)S(1)}, bf16[32,2,1280]{2,0,1:T(8,128)(2,1)}, u32[]{:S(2)}, u32[]{:S(2)}) collective-permute-start(bf16[32,2,1280]{2,0,1:T(8,128)(2,1)S(1)} %get-tuple-element.63), channel_id=1, source_target_pairs={{0,3},{1,2},{2,1},{3,0},{4,7},{5,6},{6,5},{7,4},{8,11},{9,10},{10,... | collective-permute-start | bytes 491528 | tf_op jit(solution)/shard_map/ppermute | solution.py:23
  84.5 1.5 %copy-start = (bf16[32,8,1280]{0,1,2:T(8,128)(2,1)}, bf16[32,8,1280]{0,1,2:T(8,128)(2,1)S(1)}, u32[]{:S(2)}) copy-start(bf16[32,8,1280]{0,1,2:T(8,128)(2,1)S(1)} %get-tuple-element.119) | copy-start | bytes 1966084 | tf_op jit(solution)/shard_map/while
  103.8 3.1 %copy-start.2 = (f32[8,32,640]{2,1,0:T(8,128)S(1)}, f32[8,32,640]{2,1,0:T(8,128)}, u32[]{:S(2)}) copy-start(f32[8,32,640]{2,1,0:T(8,128)} %copy.67) | copy-start | bytes 1966084 | tf_op jit(solution)/shard_map/while
  106.9 5.8 %copy-start.1 = (bf16[32,8,1280]{0,1,2:T(8,128)(2,1)S(1)}, bf16[32,8,1280]{0,1,2:T(8,128)(2,1)}, u32[]{:S(2)}) copy-start(bf16[32,8,1280]{0,1,2:T(8,128)(2,1)} %copy-done) | copy-start | bytes 1966084 | tf_op jit(solution)/shard_map/while
  112.7 1.5 %copy-start = (bf16[32,8,1280]{0,1,2:T(8,128)(2,1)}, bf16[32,8,1280]{0,1,2:T(8,128)(2,1)S(1)}, u32[]{:S(2)}) copy-start(bf16[32,8,1280]{0,1,2:T(8,128)(2,1)S(1)} %get-tuple-element.119) | copy-start | bytes 1966084 | tf_op jit(solution)/shard_map/while
  131.9 3.1 %copy-start.2 = (f32[8,32,640]{2,1,0:T(8,128)S(1)}, f32[8,32,640]{2,1,0:T(8,128)}, u32[]{:S(2)}) copy-start(f32[8,32,640]{2,1,0:T(8,128)} %copy.67) | copy-start | bytes 1966084 | tf_op jit(solution)/shard_map/while
  135.1 5.8 %copy-start.1 = (bf16[32,8,1280]{0,1,2:T(8,128)(2,1)S(1)}, bf16[32,8,1280]{0,1,2:T(8,128)(2,1)}, u32[]{:S(2)}) copy-start(bf16[32,8,1280]{0,1,2:T(8,128)(2,1)} %copy-done) | copy-start | bytes 1966084 | tf_op jit(solution)/shard_map/while
